TPU v7x, 128 devices: a whole 4x4x4 slice. The times are simulated.
128 devices in a mesh: fsdp: 32 (over y, z, core), dp: 4 (over x).
Axes of the slice: x: 4, y: 4, z: 4, core: 2. Of those that a mesh axis runs over, the one named last changes fastest.
Arguments:
- tokens: bfloat16 [4, 512, 6144], P('dp', 'fsdp'), may hold values from -6 to 6
- out_grad: bfloat16 [4, 512, 6144], P('dp', 'fsdp'), may hold values from -6 to 6
- row_prob: float32 [4, 1024], P('dp'), may hold values from 0.1 to 1
- row_token: int32 [4, 1024], P('dp'), may hold values from 0 to 512, as said below
- block_expert: int32 [4, 8], P('dp'), may hold values from 0 to 1, as said below
- w_gate: bfloat16 [2, 6144, 8192], P(None, None, 'fsdp'), may hold values from -0.078125 to 0.078125
- w_up: bfloat16 [2, 6144, 8192], P(None, None, 'fsdp'), may hold values from -0.078125 to 0.078125
- w_down: bfloat16 [2, 8192, 6144], P(None, 'fsdp'), may hold values from -0.0625 to 0.0625
Outputs:
- token_grad: bfloat16 [4, 512, 6144], P('dp', 'fsdp')
- prob_grad: float32 [4, 1024], P('dp')
- gate_grad: bfloat16 [2, 6144, 8192], P(None, 'dp', 'fsdp')
- up_grad: bfloat16 [2, 6144, 8192], P(None, 'dp', 'fsdp')
- down_grad: bfloat16 [2, 8192, 6144], P(None, 'fsdp', 'dp')
Inputs may be any that keep to these rules, and one draw needn't show every extreme that they name: `row_token`: in each group the blocks of 128 slots of expert 0 come first, then those of expert 1, then empty blocks. Within an expert's blocks the slots hold the distinct tokens routed to that expert in increasing order, then 512 in the slots left empty. Fewer than 512 tokens are routed to each expert. `block_expert`: never falling along a group; empty blocks carry expert 1.
All inputs are finite; a program needn't handle non-finite values.
Results may differ from a plain program's by a relative error of at most 0.02.
Values may be sent and summed in bfloat16 or wider, within the bound.
A program may use at most 256 MiB of HBM per device.

v0:
```python
import functools

import jax
import jax.numpy as jnp
from jax import lax
from jax.experimental import pallas as pl
from jax.experimental.pallas import tpu as pltpu
from jax.sharding import PartitionSpec as P

EXPERTS = 2
BLOCK = 128
SIDE = 4
GROUPS = 4
LOCAL = 16
SLOTS = 32
CHUNK = 128
CORE_ROWS = CHUNK // 2
PIECE = CORE_ROWS // 2
ORDER = (0, 3, 1, 2)
SEAT = (0, 2, 3, 1)
BF16 = jnp.bfloat16
F32 = jnp.float32


def dot(a, b, ca, cb):
    return lax.dot_general(a, b, (((ca,), (cb,)), ((), ())), preferred_element_type=F32)


def offset_row(i, j):
    seat = SEAT[i]
    if j == 0:
        return seat * LOCAL
    if j == 2:
        return 3 * CHUNK + seat * LOCAL
    return (1 + seat // 2) * CHUNK + (j // 2) * PIECE + (seat % 2) * LOCAL


def place():
    f = lax.axis_index("fsdp")
    return f // (2 * SIDE), (f // 2) % SIDE, f % 2


def kernel(
    tokens, out_grad, prob, w_gate, w_up, w_down,
    token_out, prob_out, gate_out, up_out, down_out, cols,
    xs, dys, wgu, wd, deltas, pair_in, half_b, half_a, stage, held, acc, acc_down,
    share_c, share_y, share_z, local_sem, send, recv,
):
    y, z, c = place()
    p = lax.axis_index("dp")
    width = xs.shape[1]
    half = width // 2
    part = width // GROUPS
    hs = wd.shape[1]
    count = [0]
    locals_ = [0]

    def device(yy, zz, cc):
        return {"fsdp": ((yy % SIDE) * SIDE + zz % SIDE) * 2 + cc}

    def at(da, db):
        return device(y + (1 - c) * da + c * db, z + c * da + (1 - c) * db, c)

    sibling = device(y, z, 1 - c)

    def over(k):
        return {"dp": (p + k) % GROUPS}

    barrier = pltpu.get_barrier_semaphore()
    peers = [at(1, 0), at(2, 0), at(3, 0), at(0, 1), at(0, 2), at(0, 3), sibling]
    peers += [over(1), over(2), over(3)]
    for peer in peers:
        pl.semaphore_signal(barrier, inc=1, device_id=peer, device_id_type=pl.DeviceIdType.MESH)
    pl.semaphore_wait(barrier, len(peers))

    unsent = []

    def copy(src, dst, to):
        n = count[0]
        count[0] += 1
        return pltpu.make_async_remote_copy(
            src_ref=src, dst_ref=dst, send_sem=send.at[n], recv_sem=recv.at[n],
            device_id=to, device_id_type=pl.DeviceIdType.MESH,
        )

    def local(src, dst):
        n = locals_[0]
        locals_[0] += 1
        return pltpu.make_async_copy(src, dst, local_sem.at[n])

    def start(one):
        one.start()
        unsent.append(one)

    def sent(ones):
        for one in ones:
            one.wait_send()
            unsent[:] = [copied for copied in unsent if copied is not one]

    core_row = pl.multiple_of(c * CORE_ROWS, CORE_ROWS)
    other_row = pl.multiple_of((1 - c) * CORE_ROWS, CORE_ROWS)

    def slot_row(i, j):
        return pl.multiple_of(core_row + offset_row(i, j), LOCAL)

    class Gather:
        def __init__(self, slot, mine, plus):
            far = 3 if plus else 1
            self.plus, self.far = plus, far
            self.a = {3: copy(mine, slot(3, 0), at(1, 0)), 1: copy(mine, slot(1, 0), at(3, 0))}
            self.a[2] = copy(slot(far, 0), slot(2, 0), at(1 if plus else 3, 0))
            self.b, self.s = {}, {}
            for i in range(SIDE):
                src = mine if i == 0 else slot(i, 0)
                self.b[i, 3] = copy(src, slot(i, 3), at(0, 1))
                self.b[i, 1] = copy(src, slot(i, 1), at(0, 3))
                self.b[i, 2] = copy(slot(i, far), slot(i, 2), at(0, 1 if plus else 3))
                for j in range(SIDE):
                    src = mine if i == 0 and j == 0 else slot(i, j)
                    self.s[i, j] = copy(src, slot(i, j), sibling)

        def begin_a(self):
            start(self.a[3])
            start(self.a[1])

        def begin_b(self):
            start(self.b[0, 3])
            start(self.b[0, 1])
            start(self.s[0, 0])

        def got_a(self, i):
            self.a[i].wait_recv()
            if i == self.far:
                start(self.a[2])
            start(self.b[i, 3])
            start(self.b[i, 1])
            start(self.s[i, 0])

        def got_b(self, i, j):
            self.b[i, j].wait_recv()
            if j == self.far:
                start(self.b[i, 2])
            start(self.s[i, j])

        def got_s(self, *slots):
            for slot in slots:
                self.s[slot].wait_recv()

        def from_chunk(self, q):
            if q == 0:
                ones = [self.a[2]] + [self.b[i, j] for i in (1, 2, 3) for j in (1, 3)]
                return ones + [self.s[i, 0] for i in (1, 2, 3)]
            if q == 3:
                return [self.s[i, 2] for i in range(SIDE)]
            ones = []
            for i in ORDER[2 * q - 2 : 2 * q]:
                ones += [self.b[i, 2], self.s[i, 1], self.s[i, 3]]
            return ones

    zero = [(i, 0) for i in range(SIDE)]
    near = [[(i, j) for i in ORDER[2 * u : 2 * u + 2] for j in (1, 3)] for u in range(2)]
    far = [(i, 2) for i in range(SIDE)]
    chunk_slots = [zero, near[0], near[1], far]

    def chunk_rows(q):
        return pl.ds(q * CHUNK, CHUNK)

    row0 = slot_row(0, 0)
    fill = [
        local(tokens, xs.at[pl.ds(row0, LOCAL)]),
        local(out_grad, dys.at[pl.ds(row0, LOCAL)]),
        local(w_gate.at[0], wgu.at[:, pl.ds(0, hs)]),
        local(w_up.at[0], wgu.at[:, pl.ds(hs, hs)]),
        local(w_down, wd),
        local(w_gate.at[1], wgu.at[:, pl.ds(2 * hs, hs)]),
        local(w_up.at[1], wgu.at[:, pl.ds(3 * hs, hs)]),
    ]
    ax = Gather(lambda i, j: xs.at[pl.ds(slot_row(i, j), LOCAL)], tokens, True)
    ad = Gather(lambda i, j: dys.at[pl.ds(slot_row(i, j), LOCAL)], out_grad, False)

    def col_slot(k):
        def slot(i, j):
            row = offset_row(i, j)
            rows = pl.ds(pl.multiple_of(core_row + row % CHUNK, LOCAL), LOCAL)
            return cols.at[k, row // CHUNK, pl.ds(1, GROUPS - 1), rows]

        return slot

    bx = Gather(col_slot(0), stage.at[0], True)
    bd = Gather(col_slot(1), stage.at[1], False)
    swaps = []
    for k, src in enumerate((tokens, out_grad)):
        for step in range(1, GROUPS):
            lane = pl.multiple_of(((p + step) % GROUPS) * part, part)
            swaps.append(
                copy(src.at[:, pl.ds(lane, part)], stage.at[k, GROUPS - step - 1], over(step))
            )

    ring, own_cols, load = {}, {}, {}
    lane = pl.multiple_of(p * part, part)
    for q in range(SIDE):
        top, bottom = pl.ds(0, CHUNK // 2), pl.ds(CHUNK // 2, CHUNK // 2)
        ring[q] = (
            copy(deltas.at[q, 0], deltas.at[q, 3], over(1)),
            copy(deltas.at[q, 0], deltas.at[q, 1], over(3)),
            copy(deltas.at[q, 3, top], deltas.at[q, 2, top], over(1)),
            copy(deltas.at[q, 1, bottom], deltas.at[q, 2, bottom], over(3)),
        )
        own_cols[q] = (
            local(xs.at[chunk_rows(q), pl.ds(lane, part)], cols.at[0, q, 0]),
            local(dys.at[chunk_rows(q), pl.ds(lane, part)], cols.at[1, q, 0]),
        )
        load[q] = local(cols.at[:, q], held)
    stage_own = [local(stage.at[k], col_slot(k)(0, 0)) for k in range(2)]

    def forward(q):
        where = chunk_rows(q)
        for e in range(EXPERTS):
            gate_up = dot(xs[where], wgu[:, 2 * e * hs : (2 * e + 2) * hs], 1, 0)
            gate, up = gate_up[:, :hs], gate_up[:, hs:]
            back = dot(dys[where], wd[e], 1, 1)
            sigma = jax.nn.sigmoid(gate)
            silu = gate * sigma
            hidden = (silu * up).astype(BF16).astype(F32)
            product = hidden * back
            folded = product[:, : hs // 2] + product[:, hs // 2 :]
            row = jnp.sum(jnp.transpose(folded), axis=0, keepdims=True)
            for k in range(2):
                for i, j in chunk_slots[q]:
                    first = k * CORE_ROWS + offset_row(i, j) % CHUNK
                    owner = device(y + (1 - k) * i + k * j, z + k * i + (1 - k) * j, k)["fsdp"]
                    share_c[c, pl.ds(owner, 1), e * LOCAL : (e + 1) * LOCAL] = row[
                        :, first : first + LOCAL
                    ]
            share = prob[where, e : e + 1]
            scaled = share * back
            slope = sigma * (1.0 + gate * (1.0 - sigma))
            deltas[q, 0, :, 2 * e * hs : (2 * e + 1) * hs] = (scaled * up * slope).astype(BF16)
            deltas[q, 0, :, (2 * e + 1) * hs : (2 * e + 2) * hs] = (scaled * silu).astype(BF16)
            deltas[q, 0, :, (4 + e) * hs : (5 + e) * hs] = (share * hidden).astype(BF16)

    def token_terms(q):
        step = 512
        where = chunk_rows(q)

        def body(n, carry):
            at_n = pl.ds(pl.multiple_of(n * step, step), step)
            total = dot(deltas[q, 0, :, 0 : 4 * hs], wgu[at_n, :], 1, 1)
            dys[where, at_n] = total.astype(BF16)
            return carry

        lax.fori_loop(0, width // step, body, 0)

    def start_own_cols(q):
        for one in own_cols[q]:
            one.start()

    def send_deltas(q):
        start(ring[q][0])
        start(ring[q][1])

    def pass_deltas(q):
        ring[q][0].wait_recv()
        start(ring[q][2])
        ring[q][1].wait_recv()
        start(ring[q][3])

    tile = 256
    drain = []

    def load_cols(q):
        bx.got_s(*chunk_slots[q])
        bd.got_s(*chunk_slots[q])
        if q == 0:
            for one in stage_own:
                one.wait()
        load[q].start()

    def weight_terms(q, first=False, last=False):
        ring[q][2].wait_recv()
        ring[q][3].wait_recv()
        load[q].wait()
        rows = GROUPS * CHUNK
        delta = deltas.at[q]

        def one_tile(n):
            lanes = pl.ds(pl.multiple_of(n * tile, tile), tile)
            x = held[0, :, :, lanes].reshape(rows, tile)
            return lanes, dot(x, delta[:, :, 0 : 4 * hs].reshape(rows, 4 * hs), 0, 0)

        def body(n, carry):
            lanes, term = one_tile(n)
            if first:
                acc[lanes, :] = term
            else:
                acc[lanes, :] += term
            return carry

        if not last:
            lax.fori_loop(0, part // tile, body, 0)
        else:
            for n in range(part // tile):
                lanes, term = one_tile(n)
                total = (acc[n * tile : (n + 1) * tile, :] + term).astype(BF16)
                up_row, left = (n % 2) * tile, (n // 2) * 4 * hs
                xs[up_row : up_row + tile, left : left + 4 * hs] = total
                for e in range(EXPERTS):
                    for k, out in enumerate((gate_out, up_out)):
                        src = xs.at[
                            pl.ds(up_row, tile), pl.ds(left + (2 * e + k) * hs, hs)
                        ]
                        drain.append(local(src, out.at[e, pl.ds(n * tile, tile)]))
                        drain[-1].start()
        for e in range(EXPERTS):
            term = dot(
                delta[:, :, (4 + e) * hs : (5 + e) * hs].reshape(rows, hs),
                held[1].reshape(rows, part), 0, 0,
            )
            if first:
                acc_down[e] = term
            elif not last:
                acc_down[e] += term
            else:
                left = 3 * 4 * hs
                xs[e * hs : (e + 1) * hs, left : left + part] = (acc_down[e] + term).astype(BF16)
                src = xs.at[pl.ds(e * hs, hs), pl.ds(left, part)]
                drain.append(local(src, down_out.at[e]))
                drain[-1].start()

    pair = [
        copy(dys.at[pl.ds(q * CHUNK + other_row, CORE_ROWS)], pair_in.at[q], sibling)
        for q in range(SIDE)
    ]
    lo, hi = pl.ds(0, half), pl.ds(half, half)

    def piece(q, u):
        return pl.ds(q * CHUNK + core_row + u * PIECE, PIECE)

    def add(rows, lanes, *others):
        def body(n, carry):
            here = pl.ds(pl.multiple_of(rows.start + n * LOCAL, LOCAL), LOCAL)
            there = pl.ds(pl.multiple_of(n * LOCAL, LOCAL), LOCAL)
            total = dys[here, lanes].astype(F32)
            for one, cut in others:
                total += one[there, cut].astype(F32)
            dys[here, lanes] = total.astype(BF16)
            return carry

        lax.fori_loop(0, rows.size // LOCAL, body, 0)

    def pair_sum(q):
        pair[q].wait_recv()
        rows = pl.ds(q * CHUNK + core_row, CORE_ROWS)
        add(rows, lo, (pair_in.at[q], lo))
        add(rows, hi, (pair_in.at[q], hi))

    whole = pl.ds(0, half)
    far_b = [
        (
            copy(dys.at[piece(3, u), lo], half_b.at[u, 0], at(0, 1)),
            copy(dys.at[piece(3, u), hi], half_b.at[u, 1], at(0, 3)),
        )
        for u in range(2)
    ]
    near_b = [
        (
            copy(dys.at[piece(1 + u, 0), hi], half_b.at[u, 2], at(0, 1)),
            copy(dys.at[piece(1 + u, 1), lo], half_b.at[u, 3], at(0, 3)),
            copy(dys.at[piece(1 + u, 0), lo], half_b.at[u, 4], at(0, 1)),
            copy(dys.at[piece(1 + u, 1), hi], half_b.at[u, 5], at(0, 3)),
        )
        for u in range(2)
    ]

    def far_to_near(u):
        far_b[u][0].wait_recv()
        add(piece(1 + u, 0), lo, (half_b.at[u, 0], whole))
        start(near_b[u][2])
        far_b[u][1].wait_recv()
        add(piece(1 + u, 1), hi, (half_b.at[u, 1], whole))
        start(near_b[u][3])

    def near_to_mine(u):
        for one in near_b[u]:
            one.wait_recv()
        add(piece(0, u), lo, (half_b.at[u, 3], whole), (half_b.at[u, 4], whole))
        add(piece(0, u), hi, (half_b.at[u, 2], whole), (half_b.at[u, 5], whole))

    def seat(i):
        return pl.ds(slot_row(i, 0), LOCAL)

    far_a = (
        copy(dys.at[seat(2), lo], half_a.at[0], at(1, 0)),
        copy(dys.at[seat(2), hi], half_a.at[1], at(3, 0)),
    )
    near_a = (
        copy(dys.at[seat(1), hi], half_a.at[2], at(1, 0)),
        copy(dys.at[seat(3), lo], half_a.at[3], at(3, 0)),
        copy(dys.at[seat(1), lo], half_a.at[4], at(1, 0)),
        copy(dys.at[seat(3), hi], half_a.at[5], at(3, 0)),
    )

    to_c = copy(share_c.at[c], share_c.at[c], sibling)
    to_y = [copy(share_y.at[y], share_y.at[y], device(y + k, z, c)) for k in range(1, SIDE)]
    to_z = [copy(share_z.at[z], share_z.at[z], device(y, z + k, c)) for k in range(1, SIDE)]

    def prob_y():
        to_c.wait_recv()
        share_y[y] = share_c[0] + share_c[1]
        for one in to_y:
            start(one)

    def prob_z():
        for one in to_y:
            one.wait_recv()
        share_z[z] = (share_y[0] + share_y[1]) + (share_y[2] + share_y[3])
        for one in to_z:
            start(one)

    def prob_end():
        for one in to_z:
            one.wait_recv()
        prob_out[...] = (share_z[0] + share_z[1]) + (share_z[2] + share_z[3])

    def near_shards(x, d, u):
        for i in ORDER[2 * u : 2 * u + 2]:
            x.got_b(i, 3)
            d.got_b(i, 1)
            x.got_b(i, 1)
            d.got_b(i, 3)

    def far_shards(x, d):
        for i in ORDER:
            x.got_b(i, 2)
            d.got_b(i, 2)

    def first_shards(x, d):
        x.got_a(3)
        d.got_a(1)
        x.got_a(1)
        d.got_a(3)

    ax.begin_a()
    ad.begin_a()
    for one in fill:
        one.start()
    for one in swaps:
        start(one)
    ax.begin_b()
    ad.begin_b()
    share_c[c] = jnp.zeros(share_c.shape[1:], F32)
    first_shards(ax, ad)
    ax.got_a(2)
    ad.got_a(2)
    for one in fill:
        one.wait()
    ax.got_s(*zero)
    ad.got_s(*zero)
    start_own_cols(0)
    forward(0)
    send_deltas(0)
    for one in swaps:
        one.wait_recv()
    for one in stage_own:
        one.start()
    bx.begin_a()
    bd.begin_a()

    near_shards(ax, ad, 0)
    ax.got_s(*near[0])
    ad.got_s(*near[0])
    start_own_cols(1)
    forward(1)
    send_deltas(1)
    near_shards(ax, ad, 1)
    bx.begin_b()
    bd.begin_b()
    first_shards(bx, bd)
    ax.got_s(*near[1])
    ad.got_s(*near[1])
    start_own_cols(2)
    forward(2)
    send_deltas(2)
    pass_deltas(0)

    far_shards(ax, ad)
    bx.got_a(2)
    bd.got_a(2)
    ax.got_s(*far)
    ad.got_s(*far)
    start_own_cols(3)
    forward(3)
    send_deltas(3)
    start(to_c)

    def token_part(q):
        sent(ad.from_chunk(q))
        for one in own_cols[q]:
            one.wait()
        token_terms(q)
        start(pair[q])

    token_part(3)
    near_shards(bx, bd, 0)
    token_part(1)
    pair_sum(3)
    for u in range(2):
        start(far_b[u][0])
        start(far_b[u][1])
    prob_y()
    pair_sum(1)
    start(near_b[0][0])
    start(near_b[0][1])
    pass_deltas(1)
    token_part(2)
    near_shards(bx, bd, 1)
    pair_sum(2)
    start(near_b[1][0])
    start(near_b[1][1])
    prob_z()
    far_to_near(0)
    far_to_near(1)
    token_part(0)
    load_cols(0)
    pass_deltas(2)
    prob_end()
    pair_sum(0)
    weight_terms(0, first=True)
    far_shards(bx, bd)
    load_cols(1)
    near_to_mine(0)
    near_to_mine(1)
    start(far_a[0])
    start(far_a[1])
    start(near_a[0])
    start(near_a[1])
    weight_terms(1)
    load_cols(2)
    far_a[0].wait_recv()
    add(seat(1), lo, (half_a.at[0], whole))
    start(near_a[2])
    far_a[1].wait_recv()
    add(seat(3), hi, (half_a.at[1], whole))
    start(near_a[3])
    pass_deltas(3)
    weight_terms(2)
    load_cols(3)
    for one in near_a:
        one.wait_recv()
    mine = dys[seat(0), lo].astype(F32)
    mine += half_a[3].astype(F32)
    mine += half_a[4].astype(F32)
    token_out[:, lo] = mine.astype(BF16)
    mine = dys[seat(0), hi].astype(F32)
    mine += half_a[2].astype(F32)
    mine += half_a[5].astype(F32)
    token_out[:, hi] = mine.astype(BF16)
    sent(list(unsent))
    weight_terms(3, last=True)
    for one in drain:
        one.wait()


COPIES = 31 * 4 + 6 + 16 + 4 + 12 + 6 + 7
LOCALS = 7 + 12 + 2 + 26


def fused(tokens, out_grad, prob, w_gate, w_up, w_down):
    local, width = tokens.shape
    hs = w_gate.shape[2]
    part = width // GROUPS
    gtok = local * SLOTS
    anywhere = pl.BlockSpec(memory_space=pl.ANY)
    vmem = pl.BlockSpec(memory_space=pltpu.VMEM)
    flops = 2 * gtok * width * hs * 16
    return pl.pallas_call(
        kernel,
        out_shape=(
            jax.ShapeDtypeStruct((local, width), BF16),
            jax.ShapeDtypeStruct((SLOTS, 128), F32),
            jax.ShapeDtypeStruct((EXPERTS, part, hs), BF16),
            jax.ShapeDtypeStruct((EXPERTS, part, hs), BF16),
            jax.ShapeDtypeStruct((EXPERTS, hs, part), BF16),
            jax.ShapeDtypeStruct((2, SIDE, GROUPS, CHUNK, part), BF16),
        ),
        in_specs=[anywhere, anywhere, vmem, anywhere, anywhere, anywhere],
        out_specs=(vmem, vmem, anywhere, anywhere, anywhere, anywhere),
        scratch_shapes=[
            pltpu.VMEM((gtok, width), BF16),
            pltpu.VMEM((gtok, width), BF16),
            pltpu.VMEM((width, 4 * hs), BF16),
            pltpu.VMEM(w_down.shape, BF16),
            pltpu.VMEM((SIDE, GROUPS, CHUNK, 6 * hs), BF16),
            pltpu.VMEM((SIDE, CORE_ROWS, width), BF16),
            pltpu.VMEM((2, 6, PIECE, width // 2), BF16),
            pltpu.VMEM((6, LOCAL, width // 2), BF16),
            pltpu.VMEM((2, GROUPS - 1, LOCAL, part), BF16),
            pltpu.VMEM((2, GROUPS, CHUNK, part), BF16),
            pltpu.VMEM((part, 4 * hs), F32),
            pltpu.VMEM((EXPERTS, hs, part), F32),
            pltpu.VMEM((2, SLOTS, 128), F32),
            pltpu.VMEM((SIDE, SLOTS, 128), F32),
            pltpu.VMEM((SIDE, SLOTS, 128), F32),
            pltpu.SemaphoreType.DMA((LOCALS,)),
            pltpu.SemaphoreType.DMA((COPIES,)),
            pltpu.SemaphoreType.DMA((COPIES,)),
        ],
        compiler_params=pltpu.CompilerParams(
            collective_id=0, has_side_effects=True, vmem_limit_bytes=62 << 20
        ),
        cost_estimate=pl.CostEstimate(flops=flops, bytes_accessed=60 << 20, transcendentals=0),
    )(tokens, out_grad, prob, w_gate, w_up, w_down)


def shards(tokens, out_grad, row_prob, row_token, block_expert, w_gate, w_up, w_down):
    local, width = tokens.shape[1:]
    gtok = local * SLOTS
    row_expert = jnp.repeat(block_expert[0], BLOCK)
    token = row_token[0]

    y, z, c = place()
    source = token // LOCAL
    off_y = (source // (2 * SIDE) - y) % SIDE
    off_z = ((source // 2) % SIDE - z) % SIDE
    core = source % 2
    i = jnp.where(core == 0, off_y, off_z)
    j = jnp.where(core == 0, off_z, off_y)
    seat = jnp.where(i == 0, 0, jnp.where(i == 3, 1, i + 1))
    near = (1 + seat // 2) * CHUNK + (j // 2) * PIECE + (seat % 2) * LOCAL
    row = jnp.where(j % 2 == 1, near, (j // 2) * 3 * CHUNK + seat * LOCAL)
    row = jnp.where(token < gtok, row + core * CORE_ROWS + token % LOCAL, gtok)
    every = jnp.arange(gtok, dtype=jnp.int32)[None, :]
    hit = row[:, None] == every
    prob = jnp.stack(
        [
            jnp.sum(jnp.where(hit & (row_expert == e)[:, None], row_prob[0][:, None], 0.0), axis=0)
            for e in range(EXPERTS)
        ],
        axis=1,
    )
    token_sum, prob_total, gate_grad, up_grad, down_grad, _ = fused(
        tokens[0], out_grad[0], prob, w_gate, w_up, w_down
    )
    prob_tok = [prob_total[:, e * LOCAL : (e + 1) * LOCAL].reshape(gtok) for e in range(EXPERTS)]
    mine = jnp.where((row_expert == 0)[:, None], prob_tok[0][None], prob_tok[1][None])
    prob_sum = jnp.sum(jnp.where(token[:, None] == every, mine, 0.0), axis=1)
    return (token_sum[None], prob_sum[None], gate_grad, up_grad, down_grad)


def solution(mesh):
    in_specs = (
        P("dp", "fsdp", None),
        P("dp", "fsdp", None),
        P("dp", None),
        P("dp", None),
        P("dp", None),
        P(None, None, "fsdp"),
        P(None, None, "fsdp"),
        P(None, "fsdp", None),
    )
    out_specs = (
        P("dp", "fsdp", None),
        P("dp", None),
        P(None, "dp", "fsdp"),
        P(None, "dp", "fsdp"),
        P(None, "fsdp", "dp"),
    )
    return jax.shard_map(shards, mesh=mesh, in_specs=in_specs, out_specs=out_specs, check_vma=False)
```

profile of v0, /device:TPU:1, one launch (start us, length us, event | category | flops | bytes accessed | tf_op | source)
XLA Modules:
  0.0 125.4 jit_solution(12737480200010046425)
XLA Ops:
  0.7 0.7 compare_bitcast_fusion
  1.3 0.1 broadcast_bitcast_fusion
  1.4 0.7 fusion.16
  2.1 2.0 %select_reduce_fusion.2 = (f32[512]{0:T(512)S(1)}, f32[512]{0:T(512)S(1)}) fusion(f32[1024]{0:T(1024)} %bitcast.21, s32[1024]{0:T(1024)S(1)} %fusion.16, pred[1024]{0:T(1024)(128)(4,1)S(1)} %get-tuple-element.22, pred[1024]{0:T(1024)(128)(4,1)S(1)} %get-tuple-element.21), kind=kLoop, calls=%fused_computation.3 | loop fusion | flops 3668992 | bytes 14336 | tf_op jit(solution)/shard_map/reduce_sum | solution.py:636
  4.2 0.9 copy.16.prob
  5.0 0.0 copy-start.2
  5.0 110.4 %shard_map.119 = (bf16[16,6144]{1,0:T(8,128)(2,1)}, f32[32,128]{1,0:T(8,128)}, bf16[2,1536,256]{2,1,0:T(8,128)(2,1)}, bf16[2,1536,256]{2,1,0:T(8,128)(2,1)}, bf1...) custom-call(bf16[16,6144]{1,0:T(8,128)(2,1)} %bitcast.23, bf16[16,6144]{1,0:T(8,128)(2,1)} %bitcast.24, ...), custom_call_target="tpu_custom_call" | custom-call | flops 25769803776 | bytes 62914560 | tf_op jit(solution)/shard_map/pallas_call | solution.py:576
  115.4 0.0 copy-start.1
  115.4 0.9 fusion.25
  116.4 0.1 broadcast_in_dim.73
  116.4 0.1 broadcast_in_dim.75
  116.5 0.0 copy-done.2
  116.5 1.5 %select_reduce_fusion = f32[1024]{0:T(1024)} fusion(f32[512]{0:T(512)S(1)} %broadcast_in_dim.75, f32[512]{0:T(512)S(1)} %broadcast_in_dim.73, s32[1024]{0:T(1024)S(1)} %bitcast.18, pred[1024]{0:T(1024)(128)(4,1)S(1)} %get-tuple-element.22), kind=kLoop, calls=%fused_computation | loop fusion | flops 2096128 | bytes 13312 | tf_op jit(solution)/shard_map/reduce_sum | solution.py:646
  118.0 1.6 %copy.21 = bf16[1,16,6144]{2,1,0:T(8,128)(2,1)} copy(bf16[1,16,6144]{2,1,0:T(8,128)(2,1)} %bitcast.16) | data formatting | bytes 393216
  119.7 2.7 %copy.22 = bf16[2,1536,256]{2,1,0:T(8,128)(2,1)} copy(bf16[2,1536,256]{2,1,0:T(8,128)(2,1)} %get-tuple-element.30) | data formatting | bytes 3145728
  122.3 0.0 copy-done.1
  122.3 0.0 copy-start
  122.3 1.1 copy.23
  123.5 0.8 copy-done
  124.3 1.1 copy.24
  (1 shorter events, 0.0 us)
Async XLA Ops:
  5.0 111.5 %copy-start.2 = (s32[1,1024]{1,0:T(1,128)S(1)}, s32[1,1024]{1,0:T(1,128)}, u32[]{:S(2)}) copy-start(s32[1,1024]{1,0:T(1,128)} %param.11) | copy-start | bytes 12292
  115.4 6.9 %copy-start.1 = (bf16[2,1536,256]{2,1,0:T(8,128)(2,1)S(1)}, bf16[2,1536,256]{2,1,0:T(8,128)(2,1)}, u32[]{:S(2)}) copy-start(bf16[2,1536,256]{2,1,0:T(8,128)(2,1)} %get-tuple-element.31) | copy-start | bytes 4718596
  122.3 2.0 %copy-start = (bf16[2,256,1536]{2,1,0:T(8,128)(2,1)S(1)}, bf16[2,256,1536]{2,1,0:T(8,128)(2,1)}, u32[]{:S(2)}) copy-start(bf16[2,256,1536]{2,1,0:T(8,128)(2,1)} %get-tuple-element.32) | copy-start | bytes 4718596
where the time goes:
time: 126 us; the launch traced here: 125 us
  Pallas kernels  110 us (87%)
  local copies, waits for them, and re-layouts  9.41 us (7%)
  other arithmetic  4.93 us (4%)
    pallas_call x1, Pallas kernels, fused(): pl.pallas_call(kernel, out_shape=(jax.ShapeDtypeStruct((local, width), BF...  110 us
    unnamed x10, local copies, waits for them, and re-layouts  7.39 us

commit v1 on v0

--- a/solution.py
+++ b/solution.py
@@ -43,7 +43,7 @@
 def kernel(
     tokens, out_grad, prob, w_gate, w_up, w_down,
     token_out, prob_out, gate_out, up_out, down_out, cols,
-    xs, dys, wgu, wd, deltas, pair_in, half_b, half_a, stage, held, acc, acc_down,
+    xs, dys, wgu, wd, deltas, pair_in, half_b, half_a, stage, held, first_tg, acc, acc_down,
     share_c, share_y, share_z, local_sem, send, recv,
 ):
     y, z, c = place()
@@ -199,18 +199,23 @@
     ring, own_cols, load = {}, {}, {}
     lane = pl.multiple_of(p * part, part)
     for q in range(SIDE):
-        top, bottom = pl.ds(0, CHUNK // 2), pl.ds(CHUNK // 2, CHUNK // 2)
-        ring[q] = (
-            copy(deltas.at[q, 0], deltas.at[q, 3], over(1)),
-            copy(deltas.at[q, 0], deltas.at[q, 1], over(3)),
-            copy(deltas.at[q, 3, top], deltas.at[q, 2, top], over(1)),
-            copy(deltas.at[q, 1, bottom], deltas.at[q, 2, bottom], over(3)),
-        )
+        ring[q] = []
+        for e in range(EXPERTS):
+            cut = pl.ds(3 * e * hs, 3 * hs)
+            here = deltas.at[q, 0, :, cut]
+            passed = deltas.at[q, (3, 1)[e], :, cut]
+            ring[q].append(
+                (
+                    copy(here, deltas.at[q, 3, :, cut], over(1)),
+                    copy(here, deltas.at[q, 1, :, cut], over(3)),
+                    copy(passed, deltas.at[q, 2, :, cut], over((1, 3)[e])),
+                )
+            )
         own_cols[q] = (
             local(xs.at[chunk_rows(q), pl.ds(lane, part)], cols.at[0, q, 0]),
             local(dys.at[chunk_rows(q), pl.ds(lane, part)], cols.at[1, q, 0]),
         )
-        load[q] = local(cols.at[:, q], held)
+        load[q] = local(cols.at[:, q], held.at[q % 2])
     stage_own = [local(stage.at[k], col_slot(k)(0, 0)) for k in range(2)]
 
     def forward(q):
@@ -235,18 +240,23 @@
             share = prob[where, e : e + 1]
             scaled = share * back
             slope = sigma * (1.0 + gate * (1.0 - sigma))
-            deltas[q, 0, :, 2 * e * hs : (2 * e + 1) * hs] = (scaled * up * slope).astype(BF16)
-            deltas[q, 0, :, (2 * e + 1) * hs : (2 * e + 2) * hs] = (scaled * silu).astype(BF16)
-            deltas[q, 0, :, (4 + e) * hs : (5 + e) * hs] = (share * hidden).astype(BF16)
-
-    def token_terms(q):
-        step = 512
-        where = chunk_rows(q)
+            terms = [scaled * up * slope, scaled * silu]
+            terms.insert(2 * e, share * hidden)
+            for k, term in enumerate(terms):
+                left = (3 * e + k) * hs
+                deltas[q, 0, :, left : left + hs] = term.astype(BF16)
+            for one in ring[q][e][:2]:
+                start(one)
+
+    def token_terms(*qs):
+        step = 1024
+        into = [first_tg if q == 0 else dys.at[chunk_rows(q)] for q in qs]
 
         def body(n, carry):
             at_n = pl.ds(pl.multiple_of(n * step, step), step)
-            total = dot(deltas[q, 0, :, 0 : 4 * hs], wgu[at_n, :], 1, 1)
-            dys[where, at_n] = total.astype(BF16)
+            both = dot(jnp.concatenate([deltas[one, 0, :, hs : 5 * hs] for one in qs], axis=0), wgu[at_n, :], 1, 1)
+            for k, one in enumerate(into):
+                one[:, at_n] = both[k * CHUNK : (k + 1) * CHUNK].astype(BF16)
             return carry
 
         lax.fori_loop(0, width // step, body, 0)
@@ -255,15 +265,10 @@
         for one in own_cols[q]:
             one.start()
 
-    def send_deltas(q):
-        start(ring[q][0])
-        start(ring[q][1])
-
     def pass_deltas(q):
-        ring[q][0].wait_recv()
-        start(ring[q][2])
-        ring[q][1].wait_recv()
-        start(ring[q][3])
+        for e in range(EXPERTS):
+            ring[q][e][e].wait_recv()
+            start(ring[q][e][2])
 
     tile = 256
     drain = []
@@ -277,16 +282,18 @@
         load[q].start()
 
     def weight_terms(q, first=False, last=False):
-        ring[q][2].wait_recv()
-        ring[q][3].wait_recv()
+        for e in range(EXPERTS):
+            ring[q][e][1 - e].wait_recv()
+            ring[q][e][2].wait_recv()
         load[q].wait()
+        mine = held.at[q % 2]
         rows = GROUPS * CHUNK
         delta = deltas.at[q]
 
         def one_tile(n):
             lanes = pl.ds(pl.multiple_of(n * tile, tile), tile)
-            x = held[0, :, :, lanes].reshape(rows, tile)
-            return lanes, dot(x, delta[:, :, 0 : 4 * hs].reshape(rows, 4 * hs), 0, 0)
+            x = mine[0, :, :, lanes].reshape(rows, tile)
+            return lanes, dot(x, delta[:, :, hs : 5 * hs].reshape(rows, 4 * hs), 0, 0)
 
         def body(n, carry):
             lanes, term = one_tile(n)
@@ -313,8 +320,8 @@
                         drain[-1].start()
         for e in range(EXPERTS):
             term = dot(
-                delta[:, :, (4 + e) * hs : (5 + e) * hs].reshape(rows, hs),
-                held[1].reshape(rows, part), 0, 0,
+                delta[:, :, 5 * e * hs : (5 * e + 1) * hs].reshape(rows, hs),
+                mine[1].reshape(rows, part), 0, 0,
             )
             if first:
                 acc_down[e] = term
@@ -327,47 +334,50 @@
                 drain.append(local(src, down_out.at[e]))
                 drain[-1].start()
 
+    def token_rows(q, row, rows):
+        if q == 0:
+            return first_tg.at[pl.ds(row, rows)]
+        return dys.at[pl.ds(q * CHUNK + row, rows)]
+
     pair = [
-        copy(dys.at[pl.ds(q * CHUNK + other_row, CORE_ROWS)], pair_in.at[q], sibling)
-        for q in range(SIDE)
+        copy(token_rows(q, other_row, CORE_ROWS), pair_in.at[q], sibling) for q in range(SIDE)
     ]
     lo, hi = pl.ds(0, half), pl.ds(half, half)
 
     def piece(q, u):
-        return pl.ds(q * CHUNK + core_row + u * PIECE, PIECE)
-
-    def add(rows, lanes, *others):
+        return token_rows(q, core_row + u * PIECE, PIECE)
+
+    def add(dst, lanes, *others):
         def body(n, carry):
-            here = pl.ds(pl.multiple_of(rows.start + n * LOCAL, LOCAL), LOCAL)
-            there = pl.ds(pl.multiple_of(n * LOCAL, LOCAL), LOCAL)
-            total = dys[here, lanes].astype(F32)
+            here = pl.ds(pl.multiple_of(n * LOCAL, LOCAL), LOCAL)
+            total = dst[here, lanes].astype(F32)
             for one, cut in others:
-                total += one[there, cut].astype(F32)
-            dys[here, lanes] = total.astype(BF16)
+                total += one[here, cut].astype(F32)
+            dst[here, lanes] = total.astype(BF16)
             return carry
 
-        lax.fori_loop(0, rows.size // LOCAL, body, 0)
+        lax.fori_loop(0, dst.shape[0] // LOCAL, body, 0)
 
     def pair_sum(q):
         pair[q].wait_recv()
-        rows = pl.ds(q * CHUNK + core_row, CORE_ROWS)
+        rows = token_rows(q, core_row, CORE_ROWS)
         add(rows, lo, (pair_in.at[q], lo))
         add(rows, hi, (pair_in.at[q], hi))
 
     whole = pl.ds(0, half)
     far_b = [
         (
-            copy(dys.at[piece(3, u), lo], half_b.at[u, 0], at(0, 1)),
-            copy(dys.at[piece(3, u), hi], half_b.at[u, 1], at(0, 3)),
+            copy(piece(3, u).at[:, lo], half_b.at[u, 0], at(0, 1)),
+            copy(piece(3, u).at[:, hi], half_b.at[u, 1], at(0, 3)),
         )
         for u in range(2)
     ]
     near_b = [
         (
-            copy(dys.at[piece(1 + u, 0), hi], half_b.at[u, 2], at(0, 1)),
-            copy(dys.at[piece(1 + u, 1), lo], half_b.at[u, 3], at(0, 3)),
-            copy(dys.at[piece(1 + u, 0), lo], half_b.at[u, 4], at(0, 1)),
-            copy(dys.at[piece(1 + u, 1), hi], half_b.at[u, 5], at(0, 3)),
+            copy(piece(1 + u, 0).at[:, hi], half_b.at[u, 2], at(0, 1)),
+            copy(piece(1 + u, 1).at[:, lo], half_b.at[u, 3], at(0, 3)),
+            copy(piece(1 + u, 0).at[:, lo], half_b.at[u, 4], at(0, 1)),
+            copy(piece(1 + u, 1).at[:, hi], half_b.at[u, 5], at(0, 3)),
         )
         for u in range(2)
     ]
@@ -387,17 +397,17 @@
         add(piece(0, u), hi, (half_b.at[u, 2], whole), (half_b.at[u, 5], whole))
 
     def seat(i):
-        return pl.ds(slot_row(i, 0), LOCAL)
+        return token_rows(0, slot_row(i, 0), LOCAL)
 
     far_a = (
-        copy(dys.at[seat(2), lo], half_a.at[0], at(1, 0)),
-        copy(dys.at[seat(2), hi], half_a.at[1], at(3, 0)),
+        copy(seat(2).at[:, lo], half_a.at[0], at(1, 0)),
+        copy(seat(2).at[:, hi], half_a.at[1], at(3, 0)),
     )
     near_a = (
-        copy(dys.at[seat(1), hi], half_a.at[2], at(1, 0)),
-        copy(dys.at[seat(3), lo], half_a.at[3], at(3, 0)),
-        copy(dys.at[seat(1), lo], half_a.at[4], at(1, 0)),
-        copy(dys.at[seat(3), hi], half_a.at[5], at(3, 0)),
+        copy(seat(1).at[:, hi], half_a.at[2], at(1, 0)),
+        copy(seat(3).at[:, lo], half_a.at[3], at(3, 0)),
+        copy(seat(1).at[:, lo], half_a.at[4], at(1, 0)),
+        copy(seat(3).at[:, hi], half_a.at[5], at(3, 0)),
     )
 
     to_c = copy(share_c.at[c], share_c.at[c], sibling)
@@ -440,16 +450,29 @@
         x.got_a(1)
         d.got_a(3)
 
+    def token_part(*qs):
+        for q in qs:
+            if q > 0:
+                sent(ad.from_chunk(q))
+                for one in own_cols[q]:
+                    one.wait()
+        token_terms(*qs)
+        for q in qs:
+            start(pair[q])
+
     ax.begin_a()
     ad.begin_a()
     for one in fill:
         one.start()
     for one in swaps:
         start(one)
+    share_c[c] = jnp.zeros(share_c.shape[1:], F32)
+    ax.got_a(3)
     ax.begin_b()
     ad.begin_b()
-    share_c[c] = jnp.zeros(share_c.shape[1:], F32)
-    first_shards(ax, ad)
+    ad.got_a(1)
+    ax.got_a(1)
+    ad.got_a(3)
     ax.got_a(2)
     ad.got_a(2)
     for one in fill:
@@ -458,31 +481,29 @@
     ad.got_s(*zero)
     start_own_cols(0)
     forward(0)
-    send_deltas(0)
     for one in swaps:
         one.wait_recv()
     for one in stage_own:
         one.start()
+
+    near_shards(ax, ad, 0)
     bx.begin_a()
     bd.begin_a()
-
-    near_shards(ax, ad, 0)
     ax.got_s(*near[0])
     ad.got_s(*near[0])
     start_own_cols(1)
     forward(1)
-    send_deltas(1)
+    pass_deltas(0)
     near_shards(ax, ad, 1)
     bx.begin_b()
     bd.begin_b()
-    first_shards(bx, bd)
     ax.got_s(*near[1])
     ad.got_s(*near[1])
     start_own_cols(2)
     forward(2)
-    send_deltas(2)
-    pass_deltas(0)
-
+    first_shards(bx, bd)
+    token_part(0, 1)
+    pass_deltas(1)
     far_shards(ax, ad)
     bx.got_a(2)
     bd.got_a(2)
@@ -490,78 +511,69 @@
     ad.got_s(*far)
     start_own_cols(3)
     forward(3)
-    send_deltas(3)
     start(to_c)
-
-    def token_part(q):
-        sent(ad.from_chunk(q))
-        for one in own_cols[q]:
-            one.wait()
-        token_terms(q)
-        start(pair[q])
-
-    token_part(3)
     near_shards(bx, bd, 0)
-    token_part(1)
+    token_part(3, 2)
+    pass_deltas(2)
     pair_sum(3)
     for u in range(2):
         start(far_b[u][0])
         start(far_b[u][1])
-    prob_y()
+    near_shards(bx, bd, 1)
     pair_sum(1)
     start(near_b[0][0])
     start(near_b[0][1])
-    pass_deltas(1)
-    token_part(2)
-    near_shards(bx, bd, 1)
     pair_sum(2)
     start(near_b[1][0])
     start(near_b[1][1])
-    prob_z()
+    prob_y()
+    for one in own_cols[0]:
+        one.wait()
+    load_cols(0)
+    load_cols(1)
+    pass_deltas(3)
+    weight_terms(0, first=True)
     far_to_near(0)
     far_to_near(1)
-    token_part(0)
-    load_cols(0)
-    pass_deltas(2)
-    prob_end()
+    prob_z()
     pair_sum(0)
-    weight_terms(0, first=True)
     far_shards(bx, bd)
-    load_cols(1)
+    load_cols(2)
+    weight_terms(1)
     near_to_mine(0)
     near_to_mine(1)
     start(far_a[0])
     start(far_a[1])
     start(near_a[0])
     start(near_a[1])
-    weight_terms(1)
-    load_cols(2)
+    load_cols(3)
+    prob_end()
+    weight_terms(2)
     far_a[0].wait_recv()
     add(seat(1), lo, (half_a.at[0], whole))
     start(near_a[2])
     far_a[1].wait_recv()
     add(seat(3), hi, (half_a.at[1], whole))
     start(near_a[3])
-    pass_deltas(3)
-    weight_terms(2)
-    load_cols(3)
+    for q in range(SIDE):
+        sent(ax.from_chunk(q))
+    weight_terms(3, last=True)
     for one in near_a:
         one.wait_recv()
-    mine = dys[seat(0), lo].astype(F32)
+    mine = seat(0)[:, lo].astype(F32)
     mine += half_a[3].astype(F32)
     mine += half_a[4].astype(F32)
     token_out[:, lo] = mine.astype(BF16)
-    mine = dys[seat(0), hi].astype(F32)
+    mine = seat(0)[:, hi].astype(F32)
     mine += half_a[2].astype(F32)
     mine += half_a[5].astype(F32)
     token_out[:, hi] = mine.astype(BF16)
     sent(list(unsent))
-    weight_terms(3, last=True)
     for one in drain:
         one.wait()
 
 
-COPIES = 31 * 4 + 6 + 16 + 4 + 12 + 6 + 7
+COPIES = 31 * 4 + 6 + 24 + 4 + 12 + 6 + 7
 LOCALS = 7 + 12 + 2 + 26
 
 
@@ -595,7 +607,8 @@
             pltpu.VMEM((2, 6, PIECE, width // 2), BF16),
             pltpu.VMEM((6, LOCAL, width // 2), BF16),
             pltpu.VMEM((2, GROUPS - 1, LOCAL, part), BF16),
-            pltpu.VMEM((2, GROUPS, CHUNK, part), BF16),
+            pltpu.VMEM((2, 2, GROUPS, CHUNK, part), BF16),
+            pltpu.VMEM((CHUNK, width), BF16),
             pltpu.VMEM((part, 4 * hs), F32),
             pltpu.VMEM((EXPERTS, hs, part), F32),
             pltpu.VMEM((2, SLOTS, 128), F32),

time: 126 us -> 114 us (0.905)
  Pallas kernels: 110 us -> 98.4 us
    pallas_call x1, Pallas kernels: 110 us -> 98.4 us  [fused(): pl.pallas_call(kernel, out_shape=(jax.ShapeDtypeStruct((local, width), BF...]
where the time goes in v1:
time: 114 us; the launch traced here: 113 us
  Pallas kernels  98.4 us (86%)
  local copies, waits for them, and re-layouts  9.41 us (8%)
  other arithmetic  4.93 us (4%)
    pallas_call x1, Pallas kernels, fused(): pl.pallas_call(kernel, out_shape=(jax.ShapeDtypeStruct((local, width), BF...  98.4 us
    unnamed x10, local copies, waits for them, and re-layouts  7.39 us

profile of v1, /device:TPU:1, one launch (start us, length us, event | category | flops | bytes accessed | tf_op | source)
XLA Modules:
  0.0 113.4 jit_solution(16711380865097437222)
XLA Ops:
  0.7 0.7 compare_bitcast_fusion
  1.3 0.1 broadcast_bitcast_fusion
  1.4 0.7 fusion.16
  2.1 2.0 %select_reduce_fusion.2 = (f32[512]{0:T(512)S(1)}, f32[512]{0:T(512)S(1)}) fusion(f32[1024]{0:T(1024)} %bitcast.21, s32[1024]{0:T(1024)S(1)} %fusion.16, pred[1024]{0:T(1024)(128)(4,1)S(1)} %get-tuple-element.22, pred[1024]{0:T(1024)(128)(4,1)S(1)} %get-tuple-element.21), kind=kLoop, calls=%fused_computation.3 | loop fusion | flops 3668992 | bytes 14336 | tf_op jit(solution)/shard_map/reduce_sum | solution.py:649
  4.2 0.9 copy.16.prob
  5.0 0.0 copy-start.2
  5.0 98.4 %shard_map.119 = (bf16[16,6144]{1,0:T(8,128)(2,1)}, f32[32,128]{1,0:T(8,128)}, bf16[2,1536,256]{2,1,0:T(8,128)(2,1)}, bf16[2,1536,256]{2,1,0:T(8,128)(2,1)}, bf1...) custom-call(bf16[16,6144]{1,0:T(8,128)(2,1)} %bitcast.23, bf16[16,6144]{1,0:T(8,128)(2,1)} %bitcast.24, ...), custom_call_target="tpu_custom_call" | custom-call | flops 25769803776 | bytes 62914560 | tf_op jit(solution)/shard_map/pallas_call | solution.py:588
  103.4 0.0 copy-start.1
  103.4 0.9 fusion.25
  104.3 0.1 broadcast_in_dim.73
  104.4 0.1 broadcast_in_dim.75
  104.5 0.0 copy-done.2
  104.5 1.5 %select_reduce_fusion = f32[1024]{0:T(1024)} fusion(f32[512]{0:T(512)S(1)} %broadcast_in_dim.75, f32[512]{0:T(512)S(1)} %broadcast_in_dim.73, s32[1024]{0:T(1024)S(1)} %bitcast.18, pred[1024]{0:T(1024)(128)(4,1)S(1)} %get-tuple-element.22), kind=kLoop, calls=%fused_computation | loop fusion | flops 2096128 | bytes 13312 | tf_op jit(solution)/shard_map/reduce_sum | solution.py:659
  106.0 1.6 %copy.21 = bf16[1,16,6144]{2,1,0:T(8,128)(2,1)} copy(bf16[1,16,6144]{2,1,0:T(8,128)(2,1)} %bitcast.16) | data formatting | bytes 393216
  107.6 2.7 %copy.22 = bf16[2,1536,256]{2,1,0:T(8,128)(2,1)} copy(bf16[2,1536,256]{2,1,0:T(8,128)(2,1)} %get-tuple-element.30) | data formatting | bytes 3145728
  110.3 0.0 copy-done.1
  110.3 0.0 copy-start
  110.3 1.1 %copy.23 = bf16[2,1536,256]{2,1,0:T(8,128)(2,1)} copy(bf16[2,1536,256]{2,1,0:T(8,128)(2,1)S(1)} %copy-done.1) | data formatting | bytes 3145728
  111.4 0.8 copy-done
  112.3 1.1 %copy.24 = bf16[2,256,1536]{2,1,0:T(8,128)(2,1)} copy(bf16[2,256,1536]{2,1,0:T(8,128)(2,1)S(1)} %copy-done) | data formatting | bytes 3145728
  (1 shorter events, 0.0 us)
Async XLA Ops:
  5.0 99.5 %copy-start.2 = (s32[1,1024]{1,0:T(1,128)S(1)}, s32[1,1024]{1,0:T(1,128)}, u32[]{:S(2)}) copy-start(s32[1,1024]{1,0:T(1,128)} %param.11) | copy-start | bytes 12292
  103.4 6.9 %copy-start.1 = (bf16[2,1536,256]{2,1,0:T(8,128)(2,1)S(1)}, bf16[2,1536,256]{2,1,0:T(8,128)(2,1)}, u32[]{:S(2)}) copy-start(bf16[2,1536,256]{2,1,0:T(8,128)(2,1)} %get-tuple-element.31) | copy-start | bytes 4718596
  110.3 2.0 %copy-start = (bf16[2,256,1536]{2,1,0:T(8,128)(2,1)S(1)}, bf16[2,256,1536]{2,1,0:T(8,128)(2,1)}, u32[]{:S(2)}) copy-start(bf16[2,256,1536]{2,1,0:T(8,128)(2,1)} %get-tuple-element.32) | copy-start | bytes 4718596

commit v2 on v1

--- a/solution.py
+++ b/solution.py
@@ -237,7 +237,8 @@
                     share_c[c, pl.ds(owner, 1), e * LOCAL : (e + 1) * LOCAL] = row[
                         :, first : first + LOCAL
                     ]
-            share = prob[where, e : e + 1]
+            shares = jnp.broadcast_to(prob[e : e + 1, where], (CHUNK, CHUNK))
+            share = jnp.transpose(shares)[:, :1]
             scaled = share * back
             slope = sigma * (1.0 + gate * (1.0 - sigma))
             terms = [scaled * up * slope, scaled * silu]
@@ -486,17 +487,17 @@
     for one in stage_own:
         one.start()
 
-    near_shards(ax, ad, 0)
     bx.begin_a()
     bd.begin_a()
+    bx.begin_b()
+    bd.begin_b()
+    near_shards(ax, ad, 0)
     ax.got_s(*near[0])
     ad.got_s(*near[0])
     start_own_cols(1)
     forward(1)
     pass_deltas(0)
     near_shards(ax, ad, 1)
-    bx.begin_b()
-    bd.begin_b()
     ax.got_s(*near[1])
     ad.got_s(*near[1])
     start_own_cols(2)
@@ -648,8 +649,7 @@
         [
             jnp.sum(jnp.where(hit & (row_expert == e)[:, None], row_prob[0][:, None], 0.0), axis=0)
             for e in range(EXPERTS)
-        ],
-        axis=1,
+        ]
     )
     token_sum, prob_total, gate_grad, up_grad, down_grad, _ = fused(
         tokens[0], out_grad[0], prob, w_gate, w_up, w_down

time: 114 us -> 113 us (level)
  no operation moved by 1% of the time
where the time goes in v2:
time: 113 us
  Pallas kernels  98.1 us (87%)
  local copies, waits for them, and re-layouts  8.55 us (8%)
  other arithmetic  5.52 us (5%)
    pallas_call x1, Pallas kernels, fused(): pl.pallas_call(kernel, out_shape=(jax.ShapeDtypeStruct((local, width), BF...  98.1 us
    unnamed x10, local copies, waits for them, and re-layouts  7.39 us

profile of v2, /device:TPU:1, one launch (start us, length us, event | category | flops | bytes accessed | tf_op | source)
XLA Modules:
  0.0 112.9 jit_solution(9567949862838184976)
XLA Ops:
  0.7 0.7 compare_bitcast_fusion
  1.3 0.1 broadcast_bitcast_fusion
  1.4 0.7 fusion.16
  2.1 2.0 %select_reduce_fusion.2 = (f32[512]{0:T(512)S(1)}, f32[512]{0:T(512)S(1)}) fusion(f32[1024]{0:T(1024)} %bitcast.21, s32[1024]{0:T(1024)S(1)} %fusion.16, pred[1024]{0:T(1024)(128)(4,1)S(1)} %get-tuple-element.22, pred[1024]{0:T(1024)(128)(4,1)S(1)} %get-tuple-element.21), kind=kLoop, calls=%fused_computation.3 | loop fusion | flops 3668992 | bytes 14336 | tf_op jit(solution)/shard_map/reduce_sum | solution.py:650
  4.1 0.6 pad_maximum_fusion.prob
  4.7 0.0 copy-start.2
  4.7 98.1 %shard_map.119 = (bf16[16,6144]{1,0:T(8,128)(2,1)}, f32[32,128]{1,0:T(8,128)}, bf16[2,1536,256]{2,1,0:T(8,128)(2,1)}, bf16[2,1536,256]{2,1,0:T(8,128)(2,1)}, bf1...) custom-call(bf16[16,6144]{1,0:T(8,128)(2,1)} %bitcast.23, bf16[16,6144]{1,0:T(8,128)(2,1)} %bitcast.24, ...), custom_call_target="tpu_custom_call" | custom-call | flops 25769803776 | bytes 62914560 | tf_op jit(solution)/shard_map/pallas_call | solution.py:589
  102.8 0.0 copy-start.1
  102.9 0.9 fusion.25
  103.8 0.1 broadcast_in_dim.73
  103.9 0.1 broadcast_in_dim.75
  103.9 0.0 copy-done.2
  103.9 1.5 %select_reduce_fusion = f32[1024]{0:T(1024)} fusion(f32[512]{0:T(512)S(1)} %broadcast_in_dim.75, f32[512]{0:T(512)S(1)} %broadcast_in_dim.73, s32[1024]{0:T(1024)S(1)} %bitcast.18, pred[1024]{0:T(1024)(128)(4,1)S(1)} %get-tuple-element.22), kind=kLoop, calls=%fused_computation | loop fusion | flops 2096128 | bytes 13312 | tf_op jit(solution)/shard_map/reduce_sum | solution.py:659
  105.5 1.6 %copy.17 = bf16[1,16,6144]{2,1,0:T(8,128)(2,1)} copy(bf16[1,16,6144]{2,1,0:T(8,128)(2,1)} %bitcast.16) | data formatting | bytes 393216
  107.1 2.7 %copy.18 = bf16[2,1536,256]{2,1,0:T(8,128)(2,1)} copy(bf16[2,1536,256]{2,1,0:T(8,128)(2,1)} %get-tuple-element.30) | data formatting | bytes 3145728
  109.7 0.0 copy-done.1
  109.7 0.0 copy-start
  109.7 1.1 %copy.19 = bf16[2,1536,256]{2,1,0:T(8,128)(2,1)} copy(bf16[2,1536,256]{2,1,0:T(8,128)(2,1)S(1)} %copy-done.1) | data formatting | bytes 3145728
  110.9 0.8 copy-done
  111.7 1.1 %copy.20 = bf16[2,256,1536]{2,1,0:T(8,128)(2,1)} copy(bf16[2,256,1536]{2,1,0:T(8,128)(2,1)S(1)} %copy-done) | data formatting | bytes 3145728
Async XLA Ops:
  4.7 99.2 %copy-start.2 = (s32[1,1024]{1,0:T(1,128)S(1)}, s32[1,1024]{1,0:T(1,128)}, u32[]{:S(2)}) copy-start(s32[1,1024]{1,0:T(1,128)} %param.11) | copy-start | bytes 12292
  102.8 6.9 %copy-start.1 = (bf16[2,1536,256]{2,1,0:T(8,128)(2,1)S(1)}, bf16[2,1536,256]{2,1,0:T(8,128)(2,1)}, u32[]{:S(2)}) copy-start(bf16[2,1536,256]{2,1,0:T(8,128)(2,1)} %get-tuple-element.31) | copy-start | bytes 4718596
  109.7 2.0 %copy-start = (bf16[2,256,1536]{2,1,0:T(8,128)(2,1)S(1)}, bf16[2,256,1536]{2,1,0:T(8,128)(2,1)}, u32[]{:S(2)}) copy-start(bf16[2,256,1536]{2,1,0:T(8,128)(2,1)} %get-tuple-element.32) | copy-start | bytes 4718596
